TPU v7x, 32 devices: a whole 2x2x4 slice. The times are simulated.
32 devices in a mesh: groups: 2 (over y), hidden: 4 (over x, core), dp: 4 (over z).
Axes of the slice: x: 2, y: 2, z: 4, core: 2. Of those that a mesh axis runs over, the one named last changes fastest.
Arguments:
- activations: bfloat16 [3072, 16384], P(('groups', 'dp'), 'hidden'), parts along dimension 0, may hold values from -6 to 6
- response_mask: int32 [3072], P(('groups', 'dp')), parts along dimension 0, may hold values from 0 to 1, as said below
- seq_lengths: int32 [8, 8], P(('groups', 'dp')), parts along dimension 0, may hold values from 1 to 96, as said below
Outputs:
- factor: float32 [32768, 4, 4096], P(('groups', 'hidden'), None, 'dp'), parts along dimension 0
There are 2 independent parts, one for each index of `groups`. A program takes and returns all parts, laid end to end along the dimension named above; each array names one. Nothing has to cross between parts.
Inputs may be any that keep to these rules, and one draw needn't show every extreme that they name: `seq_lengths`: each row sums to 384; its largest entry is exactly 96 and its smallest is 1. In each index of dp, one or more sequences have no token with response_mask 1, and one or more have a token with response_mask 1.
All inputs are finite; a program needn't handle non-finite values.
Results may differ from a plain program's by a relative error of at most 0.0017.
Values may be sent and summed in bfloat16 or wider, within the bound.
A program may use at most 320 MiB of HBM per device.

v0:
```python
import jax
import jax.numpy as jnp
from jax import lax
from jax.sharding import PartitionSpec as P


def token_weights(flags, lengths):
    ends = jnp.cumsum(lengths)
    starts = ends - lengths
    places = jnp.arange(flags.shape[0], dtype=jnp.int32)[:, None]
    member = ((places >= starts[None, :]) & (places < ends[None, :])).astype(jnp.float32)
    marks = flags.astype(jnp.float32)
    counts = jnp.sum(member * marks[:, None], axis=0)
    inverse = 1.0 / jnp.maximum(counts, 1.0)
    return marks * jnp.sum(member * inverse[None, :], axis=1)


def contract_rows(left, right):
    return lax.dot_general(
        left, right, (((0,), (0,)), ((), ())), preferred_element_type=jnp.float32
    )


def per_device(activations, response_mask, seq_lengths):
    tok_rows, width = activations.shape
    n_hidden = lax.axis_size("hidden")
    n_data = lax.axis_size("dp")
    sub_width = width // n_data
    weight = token_weights(response_mask, seq_lengths.reshape(-1))
    weighted = (weight[:, None] * activations.astype(jnp.float32)).astype(jnp.bfloat16)
    weight_sum = lax.psum(jnp.sum(weight), "dp")
    split_sets = activations.reshape(tok_rows, n_data, sub_width)
    owned = lax.all_to_all(split_sets, "dp", split_axis=1, concat_axis=0, tiled=True)
    owned = owned.reshape(tok_rows * n_data, sub_width)
    column_panel = lax.all_gather(owned, "hidden", axis=1, tiled=True)
    gram = contract_rows(lax.all_gather(weighted, "dp", axis=0, tiled=True), column_panel)
    return (gram / weight_sum).reshape(width, n_hidden, sub_width)


def solution(mesh):
    placed = (P(("groups", "dp"), "hidden"), P(("groups", "dp")), P(("groups", "dp"), None))
    return jax.shard_map(
        per_device,
        mesh=mesh,
        in_specs=placed,
        out_specs=P(("groups", "hidden"), None, "dp"),
        check_vma=False,
    )
```

profile of v0, /device:TPU:25, one launch (start us, length us, event | category | flops | bytes accessed | tf_op | source)
XLA Modules:
  0.0 529.9 jit_solution(7421163100325967150)
XLA Ops:
  6.5 0.0 all-gather.3.cloned.1.call-start
  6.5 0.8 reduce-window.4
  7.4 0.7 fusion.1
  8.0 0.7 convert_element_type.10
  8.7 0.2 select_reduce_fusion.1
  8.9 0.1 select_reduce_fusion
  9.0 1.3 fusion.2
  10.3 4.6 multiply_convert_fusion
  14.8 0.0 all-gather.3.cloned.1.call-update
  14.8 0.0 all-gather.5.cloned.1.call-start
  14.9 4.6 copy.9
  19.5 154.9 %all_to_all.15 = bf16[384,4,1024]{0,2,1:T(8,128)(2,1)S(1)} all-to-all(bf16[384,4,1024]{0,2,1:T(8,128)(2,1)} %bitcast.18), channel_id=1, replica_groups=mesh['groups'=2,'hidden'=4,'dp'=4] {'dp'}, dimensions={1} | all-to-all | bytes 6291456 | tf_op jit(solution)/shard_map/all_to_all | solution.py:33
  174.5 2.9 copy.10
  177.4 0.0 all-gather.5.cloned.1.call-update
  177.4 18.0 %psum.7 = f32[]{:T(128)} all-reduce(f32[]{:T(128)} %get-tuple-element.5), channel_id=1, replica_groups=mesh['groups'=2,'hidden'=4,'dp'=4] {'dp'}, use_global_device_ids=true, to_apply=%region_4.5 | all-reduce | flops 1 | bytes 8 | tf_op jit(solution)/shard_map/psum | solution.py:31
  195.4 100.7 %all-gather.3.cloned.1.call-done = bf16[1536,4096]{1,0:T(8,128)(2,1)} async-done(((bf16[384,4096]{1,0:T(8,128)(2,1)}), bf16[1536,4096]{1,0:T(8,128)(2,1)}) %all-gather.3.cloned.1.call-update) | async-done | bytes 12582928 | tf_op jit(solution)/shard_map/all_gather | solution.py:36
  296.1 84.9 %all-gather.5.cloned.1.call-done = bf16[1536,4096]{1,0:T(8,128)(2,1)} async-done(((bf16[1536,1024]{1,0:T(8,128)(2,1)}), bf16[1536,4096]{1,0:T(8,128)(2,1)}) %all-gather.5.cloned.1.call-update) | async-done | bytes 12582928 | tf_op jit(solution)/shard_map/all_gather | solution.py:35
  381.0 63.4 %convolution_divide_fusion = f32[4096,4096]{0,1:T(8,128)} fusion(bf16[1536,4096]{1,0:T(8,128)(2,1)} %all-gather.3.cloned.1.call-done, bf16[1536,4096]{1,0:T(8,128)(2,1)} %all-gather.5.cloned.1.call-done, f32[]{:T(128)} %psum.7), kind=kOutput, calls=%fused_computation | convolution fusion | flops 51556384768 | bytes 92274688 | tf_op jit(solution)/shard_map/dot_general | solution.py:19
  444.4 78.6 %copy.11 = f32[4096,4,1024]{2,1,0:T(4,128)} copy(f32[4096,4,1024]{0,2,1:T(8,128)} %bitcast.8) | data formatting | bytes 134217728 | tf_op jit(solution)/shard_map/reshape | solution.py:37
  (1 shorter events, 0.0 us)
Async XLA Ops:
  6.5 289.6 %all-gather.3.cloned.1.call-start = ((), (), s32[]{:S(2)}) async-start(), calls=%async_computation.1 | async-start | bytes 15728640 | tf_op jit(solution)/shard_map/all_gather | solution.py:36
  14.8 366.2 %all-gather.5.cloned.1.call-start = ((), (), s32[]{:S(2)}) async-start(), calls=%async_computation.2 | async-start | bytes 15728640 | tf_op jit(solution)/shard_map/all_gather | solution.py:35
Sparse Core Ops, SparseCore 0:
  15.0 281.0 all-gather.2
  297.7 83.3 all-gather.4
where the time goes:
time: 533 us; the launch traced here: 530 us
  waiting for transfers between devices  186 us (35%)
  blocking collectives  173 us (32%)
  local copies, waits for them, and re-layouts  86.2 us (16%)
  matrix products  63.4 us (12%)
  between operations  13.4 us (3%)
  other arithmetic  8.28 us (2%)
    all_to_all x1, blocking collectives, per_device(): lax.all_to_all(split_sets, 'dp', split_axis=1, concat_axis=0, tiled=True)  155 us
    all_gather x1, waiting for transfers between devices, per_device(): lax.all_gather(weighted, 'dp', axis=0, tiled=True)  101 us
    all_gather x1, waiting for transfers between devices, per_device(): column_panel = lax.all_gather(owned, 'hidden', axis=1, tiled=True)  84.9 us
    reshape x1, local copies, waits for them, and re-layouts, per_device(): return (gram / weight_sum).reshape(width, n_hidden, sub_width)  78.6 us
    dot_general x1, matrix products, contract_rows(): lax.dot_general(left, right, (((0,), (0,)), ((), ())), preferred_element_...  63.4 us
    psum x1, blocking collectives, per_device(): weight_sum = lax.psum(jnp.sum(weight), 'dp')  18 us
  transfers between devices with their start and end apart: 2, of which 2 were waited for; matrix products, arithmetic and copies ran while one was open for 1% of the time, Pallas kernels for 0%

commit v1 on v0

v1 whole, which is shorter than its diff:
```python
import functools

import jax
import jax.numpy as jnp
from jax import lax
from jax.experimental import pallas as pl
from jax.experimental.pallas import tpu as pltpu
from jax.sharding import PartitionSpec as P


def token_weights(flags, lengths):
    ends = jnp.cumsum(lengths)
    starts = ends - lengths
    places = jnp.arange(flags.shape[0], dtype=jnp.int32)[:, None]
    member = ((places >= starts[None, :]) & (places < ends[None, :])).astype(jnp.float32)
    marks = flags.astype(jnp.float32)
    counts = jnp.sum(member * marks[:, None], axis=0)
    inverse = 1.0 / jnp.maximum(counts, 1.0)
    return marks * jnp.sum(member * inverse[None, :], axis=1)


def gram_kernel(n_hidden, n_in, place_ref, total_ref, left_ref, *rest):
    panels, out_ref, turned = rest[:n_hidden], rest[n_in], rest[n_in + 1]
    scale = 1.0 / total_ref[0]
    rows = out_ref.shape[0]
    tile = min(256, rows)

    @pl.when(pl.program_id(0) == 0)
    def _():
        for r in range(0, rows, tile):
            turned[r : r + tile, :] = left_ref[:, r : r + tile].T

    @pl.loop(0, rows // tile)
    def _(r):
        here = pl.ds(pl.multiple_of(r * tile, tile), tile)
        for k in range(n_hidden):
            acc = jnp.dot(turned[here, :], panels[k][...], preferred_element_type=jnp.float32)
            out_ref[here, k, :] = acc * scale


def gram_rows(place, total, left, panel, prev, rows):
    tokens, sub = left.shape
    n_hidden = panel.shape[1] // sub
    tile = min(256, sub)
    steps = sub // tile

    def block_of(k, j, place):
        return (0, k * steps + j)

    in_specs = [
        pl.BlockSpec(memory_space=pltpu.SMEM),
        pl.BlockSpec((tokens, sub), lambda j, place: (0, 0), pipeline_mode=pl.Buffered(1)),
    ]
    in_specs += [
        pl.BlockSpec((tokens, tile), functools.partial(block_of, k)) for k in range(n_hidden)
    ]
    operands = [place, total, left] + [panel] * n_hidden
    aliases = {}
    if prev is not None:
        in_specs.append(pl.BlockSpec(memory_space=pl.ANY))
        aliases = {len(operands): 0}
        operands.append(prev)
    return pl.pallas_call(
        functools.partial(gram_kernel, n_hidden, len(in_specs) - 2),
        out_shape=jax.ShapeDtypeStruct((rows, n_hidden, sub), jnp.float32),
        grid_spec=pltpu.PrefetchScalarGridSpec(
            num_scalar_prefetch=1,
            grid=(steps,),
            in_specs=in_specs,
            out_specs=pl.BlockSpec((sub, n_hidden, tile), lambda j, place: (place[0], 0, j)),
            scratch_shapes=[pltpu.VMEM((sub, tokens), jnp.bfloat16)],
        ),
        input_output_aliases=aliases,
        compiler_params=pltpu.CompilerParams(vmem_limit_bytes=40 * 1024 * 1024),
        cost_estimate=pl.CostEstimate(
            flops=2 * tokens * sub * n_hidden * sub,
            bytes_accessed=4 * sub * n_hidden * sub + 2 * tokens * sub * (n_hidden + 1),
            transcendentals=0,
        ),
    )(*operands)


def exchange_hidden(mine, n_hidden):
    have = {0: mine}
    step = n_hidden // 2
    while step:
        pairs = [(i, i ^ step) for i in range(n_hidden)]
        for r in list(have):
            have[r ^ step] = lax.ppermute(have[r], "hidden", pairs)
        step //= 2
    return [have[r] for r in range(n_hidden)]


def assemble_kernel(n, n_hidden, hidden_ref, *rest):
    pieces, panel, sems = rest[: n * n_hidden], rest[-2], rest[-1]
    tok, sub = pieces[0].shape
    copies = []
    for s in range(n):
        for r in range(n_hidden):
            k = lax.bitwise_xor(hidden_ref[0], jnp.int32(r))
            copies.append(
                pltpu.make_async_copy(
                    pieces[s * n_hidden + r],
                    panel.at[pl.ds(s * tok, tok), pl.ds(pl.multiple_of(k * sub, sub), sub)],
                    sems.at[s * n_hidden + r],
                )
            )
    for copy in copies:
        copy.start()
    for copy in copies:
        copy.wait()


def assemble(hidden, pieces, n, n_hidden):
    tok, sub = pieces[0].shape
    return pl.pallas_call(
        functools.partial(assemble_kernel, n, n_hidden),
        out_shape=jax.ShapeDtypeStruct((n * tok, n_hidden * sub), pieces[0].dtype),
        in_specs=[pl.BlockSpec(memory_space=pltpu.SMEM)]
        + [pl.BlockSpec(memory_space=pltpu.VMEM)] * len(pieces),
        out_specs=pl.BlockSpec(memory_space=pl.ANY),
        scratch_shapes=[pltpu.SemaphoreType.DMA((len(pieces),))],
        compiler_params=pltpu.CompilerParams(vmem_limit_bytes=24 * 1024 * 1024),
        cost_estimate=pl.CostEstimate(
            flops=0, bytes_accessed=4 * n * tok * n_hidden * sub, transcendentals=0
        ),
    )(hidden, *pieces)


def per_device(activations, response_mask, seq_lengths):
    tok, width = activations.shape
    n_hidden = lax.axis_size("hidden")
    n = lax.axis_size("dp")
    me = lax.axis_index("dp")
    sub = width // n

    weight = token_weights(response_mask, seq_lengths.reshape(-1))
    def own(c):
        return lax.dynamic_slice(activations, (0, lax.rem(c + 2 * n, n) * sub), (tok, sub))

    *mine, weight = lax.optimization_barrier([own(me + m) for m in range(n)] + [weight])
    slot_weights = [weight] + [
        lax.ppermute(weight, "dp", [(i, (i + s) % n) for i in range(n)]) for s in range(1, n)
    ]
    total = sum(jnp.sum(w) for w in slot_weights).reshape(1)

    up_pairs = [(i, i + 1) for i in range(n - 1)]
    down_pairs = [(i + 1, i) for i in range(n - 1)]
    low = [dict(enumerate(mine))] + [{} for _ in range(1, n)]
    high = [dict(enumerate(mine))] + [{} for _ in range(1, n)]
    upper = me >= n // 2

    def piece(s, p):
        a, b = p, (-p) % n
        if s == 0:
            return mine[a] if a == b else jnp.where(upper, mine[a], mine[b])

        def at(m):
            return jnp.where(me >= s, low[s][m], high[n - s][m])

        return at(a) if a == b else jnp.where(upper, at(a), at(b))

    columns, crossed, crossed_at = {}, {}, {}

    def cross(s):
        columns[s] = lax.optimization_barrier(piece(s, 0))
        crossed[s] = exchange_hidden(columns[s], n_hidden)

    cross(0)
    order = [(s, d - s) for d in range(1, 2 * n - 1) for s in range(1, n) if 0 <= d - s < n]
    window = 3
    ups, downs, waited = [], [], set()
    for i, (s, q) in enumerate(order):
        after_up = ups[i - window : i - window + 1] if i >= window else []
        after_down = downs[i - window : i - window + 1] if i >= window else []
        for slot in sorted(crossed):
            if slot not in waited and crossed_at.get(slot, 0) + 2 * window <= i + 1:
                waited.add(slot)
                after_up = after_up + crossed[slot][n_hidden // 2 : n_hidden // 2 + 1]
        m = q
        source = low[s - 1][(m + 1) % n]
        if after_up:
            source = lax.optimization_barrier([source] + after_up)[0]
        low[s][m] = lax.ppermute(source, "dp", [x for x in up_pairs if x[0] >= s - 1])
        ups.append(low[s][m])
        m = (-q) % n
        source = high[s - 1][(m - 1) % n]
        if after_down:
            source = lax.optimization_barrier([source] + after_down)[0]
        high[s][m] = lax.ppermute(source, "dp", [x for x in down_pairs if x[0] <= n - s])
        downs.append(high[s][m])
        for slot in range(1, n):
            if slot not in crossed and 0 in low[slot] and 0 in high[n - slot]:
                cross(slot)
                crossed_at[slot] = i

    hidden = lax.axis_index("hidden").astype(jnp.int32)
    spread = [x for s in range(n) for x in crossed[s]]
    panel = assemble(hidden.reshape(1), spread, n, n_hidden)

    out = None
    for p in range(n):
        left = jnp.concatenate(
            [
                (slot_weights[s][:, None] * (piece(s, p) if p else columns[s]).astype(jnp.float32)).astype(jnp.bfloat16)
                for s in range(n)
            ],
            axis=0,
        )
        chunk = lax.rem(jnp.where(upper, me + p, me + (-p) % n), n)
        place = chunk.reshape(1).astype(jnp.int32)
        out = gram_rows(place, total, left, panel, out, width)
    return out


def solution(mesh):
    placed = (P(("groups", "dp"), "hidden"), P(("groups", "dp")), P(("groups", "dp"), None))
    return jax.shard_map(
        per_device,
        mesh=mesh,
        in_specs=placed,
        out_specs=P(("groups", "hidden"), None, "dp"),
        check_vma=False,
    )
```

time: 533 us -> 351 us (0.66)
  blocking collectives: 173 us -> 0 us
  Pallas kernels: 0 us -> 96.1 us
  local copies, waits for them, and re-layouts: 86.2 us -> 9.3 us
  starting transfers between devices: 0.04 us -> 76.4 us
  matrix products: 63.4 us -> 0 us
  waiting for transfers between devices: 186 us -> 138 us
  other arithmetic: 8.28 us -> 27.8 us
  between operations: 13.4 us -> 3.06 us
    all_gather x2 -> x0, waiting for transfers between devices: 186 us -> none  [the longest x1 101 us: per_device(): lax.all_gather(weighted, 'dp', axis=0, tiled=True)]
    all_to_all x1 -> x0, blocking collectives: 155 us -> none  [per_device(): lax.all_to_all(split_sets, 'dp', split_axis=1, concat_axis=0, tiled=True)]
    ppermute x0 -> x39, waiting for transfers between devices: none -> 138 us  [the longest x12 111 us: per_device(): lax.ppermute(source, 'dp', [x for x in up_pairs if x[0] >= s - 1])]
    pallas_call x0 -> x5, Pallas kernels: none -> 96.1 us  [the longest x4 93.6 us: gram_rows(): pl.pallas_call(functools.partial(gram_kernel, n_hidden, len(in_specs) - 2...]
    reshape x1 -> x0, local copies, waits for them, and re-layouts: 78.6 us -> none  [per_device(): return (gram / weight_sum).reshape(width, n_hidden, sub_width)]
    ppermute x0 -> x39, starting transfers between devices: none -> 76.4 us  [the longest x12 26.7 us: per_device(): lax.ppermute(source, 'dp', [x for x in down_pairs if x[0] <= n - s])]
    dot_general x1 -> x0, matrix products: 63.4 us -> none  [contract_rows(): lax.dot_general(left, right, (((0,), (0,)), ((), ())), preferred_element_...]
    psum x1 -> x0, blocking collectives: 18 us -> none  [per_device(): weight_sum = lax.psum(jnp.sum(weight), 'dp')]
  transfers between devices with their start and end apart: 2 -> 39, of which waited for: 2 -> 11; matrix products, arithmetic and copies ran while one was open for 1% -> 7% of each run, Pallas kernels for 0% -> 0%
where the time goes in v1:
time: 351 us; the launch traced here: 350 us
  waiting for transfers between devices  138 us (39%)
  Pallas kernels  96.1 us (27%)
  starting transfers between devices  76.4 us (22%)
  other arithmetic  27.8 us (8%)
  local copies, waits for them, and re-layouts  9.3 us (3%)
    ppermute x12, waiting for transfers between devices, per_device(): lax.ppermute(source, 'dp', [x for x in up_pairs if x[0] >= s - 1])  111 us
    pallas_call x4, Pallas kernels, gram_rows(): pl.pallas_call(functools.partial(gram_kernel, n_hidden, len(in_specs) - 2...  93.6 us
    ppermute x12, starting transfers between devices, per_device(): lax.ppermute(source, 'dp', [x for x in down_pairs if x[0] <= n - s])  26.7 us
    ppermute x12, starting transfers between devices, exchange_hidden(): have[r ^ step] = lax.ppermute(have[r], 'hidden', pairs)  20.8 us
    ppermute x12, waiting for transfers between devices, per_device(): lax.ppermute(source, 'dp', [x for x in down_pairs if x[0] <= n - s])  19.3 us
    convert_element_type x4, other arithmetic, per_device(): (slot_weights[s][:, None] * (piece(s, p) if p else columns[s]).astype(jnp...  16.5 us
    ppermute x12, starting transfers between devices, per_device(): lax.ppermute(source, 'dp', [x for x in up_pairs if x[0] >= s - 1])  15.4 us
    ppermute x3, starting transfers between devices, per_device(): lax.ppermute(weight, 'dp', [(i, (i + s) % n) for i in range(n)])  13.5 us
  transfers between devices with their start and end apart: 39, of which 11 were waited for; matrix products, arithmetic and copies ran while one was open for 7% of the time, Pallas kernels for 0%

profile of v1, /device:TPU:25, one launch (start us, length us, event | category | flops | bytes accessed | tf_op | source)
XLA Modules:
  0.0 350.4 jit_solution(11908248702313266343)
XLA Ops:
  0.0 0.8 reduce-window.4
  3.1 3.4 constant_dynamic-slice_fusion
  6.5 2.1 collective-permute-start.6
  8.6 1.3 collective-permute-start.3
  9.9 1.3 collective-permute-start.15
  11.2 4.7 %collective-permute-start.9 = (bf16[384,1024]{1,0:T(8,128)(2,1)S(1)}, bf16[384,1024]{1,0:T(8,128)(2,1)S(1)}, u32[]{:S(2)}, u32[]{:S(2)}) collective-permute-start(bf16[384,1024]{1,0:T(8,128)(2,1)S(1)} %get-tuple-element.36), channel_id=1, source_target_pairs={{1,0},{2,1},{3,2},{5,4},{6,5},{7,6},{9,8},{10,9},{11,10},{13,12},{... | collective-permute-start | bytes 2359304 | tf_op jit(solution)/shard_map/ppermute | solution.py:190
  15.9 9.2 %collective-permute-done.6 = bf16[384,1024]{1,0:T(8,128)(2,1)S(1)} collective-permute-done((bf16[384,1024]{1,0:T(8,128)(2,1)}, bf16[384,1024]{1,0:T(8,128)(2,1)S(1)}, u32[]{:S(2)}, u32[]{:S(2)}) %collective-permute-start.6) | collective-permute-done | bytes 786464 | tf_op jit(solution)/shard_map/ppermute | solution.py:190
  25.1 4.1 %collective-permute-start.7 = (bf16[384,1024]{1,0:T(8,128)(2,1)}, bf16[384,1024]{1,0:T(8,128)(2,1)S(1)}, u32[]{:S(2)}, u32[]{:S(2)}) collective-permute-start(bf16[384,1024]{1,0:T(8,128)(2,1)} %get-tuple-element.34), channel_id=1, source_target_pairs={{1,0},{2,1},{3,2},{5,4},{6,5},{7,6},{9,8},{10,9},{11,10},{13,12},{... | collective-permute-start | bytes 2359304 | tf_op jit(solution)/shard_map/ppermute | solution.py:190
  29.3 1.3 collective-permute-start.4
  30.6 15.2 %collective-permute-done.15 = bf16[384,1024]{1,0:T(8,128)(2,1)} collective-permute-done((bf16[384,1024]{1,0:T(8,128)(2,1)S(1)}, bf16[384,1024]{1,0:T(8,128)(2,1)}, u32[]{:S(2)}, u32[]{:S(2)}) %collective-permute-start.15) | collective-permute-done | bytes 786464 | tf_op jit(solution)/shard_map/ppermute | solution.py:184
  45.8 1.3 collective-permute-start.20
  47.1 1.6 collective-permute-start.12
  48.7 10.1 %collective-permute-done.7 = bf16[384,1024]{1,0:T(8,128)(2,1)S(1)} collective-permute-done((bf16[384,1024]{1,0:T(8,128)(2,1)}, bf16[384,1024]{1,0:T(8,128)(2,1)S(1)}, u32[]{:S(2)}, u32[]{:S(2)}) %collective-permute-start.7) | collective-permute-done | bytes 786464 | tf_op jit(solution)/shard_map/ppermute | solution.py:190
  58.8 5.0 %collective-permute-start.8 = (bf16[384,1024]{1,0:T(8,128)(2,1)S(1)}, bf16[384,1024]{1,0:T(8,128)(2,1)}, u32[]{:S(2)}, u32[]{:S(2)}) collective-permute-start(bf16[384,1024]{1,0:T(8,128)(2,1)S(1)} %get-tuple-element.35.rest_0_), channel_id=1, source_target_pairs={{1,0},{2,1},{3,2},{5,4},{6,5},{7,6},{9,8},{10,9},{11,10},{13,12},{... | collective-permute-start | bytes 2359304 | tf_op jit(solution)/shard_map/ppermute | solution.py:190
  63.8 1.2 collective-permute-start.23
  65.0 1.3 collective-permute-start.5
  66.3 13.2 %collective-permute-done.20 = bf16[384,1024]{1,0:T(8,128)(2,1)} collective-permute-done((bf16[384,1024]{1,0:T(8,128)(2,1)}, bf16[384,1024]{1,0:T(8,128)(2,1)}, u32[]{:S(2)}, u32[]{:S(2)}) %collective-permute-start.20) | collective-permute-done | bytes 786464 | tf_op jit(solution)/shard_map/ppermute | solution.py:184
  79.5 1.3 collective-permute-start.18
  80.8 0.7 collective-permute-start.10
  81.5 1.2 broadcast_select_fusion.6.rest_8_
  82.8 1.3 collective-permute-start.21
  84.1 1.6 collective-permute-start.11
  85.6 0.7 collective-permute-start.13
  86.3 26.8 %collective-permute-done.18 = bf16[384,1024]{1,0:T(8,128)(2,1)S(1)} collective-permute-done((bf16[384,1024]{1,0:T(8,128)(2,1)}, bf16[384,1024]{1,0:T(8,128)(2,1)S(1)}, u32[]{:S(2)}, u32[]{:S(2)}) %collective-permute-start.18) | collective-permute-done | bytes 786464 | tf_op jit(solution)/shard_map/ppermute | solution.py:184
  113.1 1.3 collective-permute-start.24
  114.4 1.2 copy-done.3
  115.6 1.3 collective-permute-start.22
  116.9 1.6 collective-permute-start.19
  118.5 1.6 collective-permute-start.14
  120.1 12.1 %collective-permute-done.24 = bf16[384,1024]{1,0:T(8,128)(2,1)S(1)} collective-permute-done((bf16[384,1024]{1,0:T(8,128)(2,1)S(1)}, bf16[384,1024]{1,0:T(8,128)(2,1)S(1)}, u32[]{:S(2)}, u32[]{:S(2)}) %collective-permute-start.24) | collective-permute-done | bytes 786464 | tf_op jit(solution)/shard_map/ppermute | solution.py:184
  132.2 17.0 %collective-permute-done.22 = bf16[384,1024]{1,0:T(8,128)(2,1)} collective-permute-done((bf16[384,1024]{1,0:T(8,128)(2,1)S(1)}, bf16[384,1024]{1,0:T(8,128)(2,1)}, u32[]{:S(2)}, u32[]{:S(2)}) %collective-permute-start.22) | collective-permute-done | bytes 786464 | tf_op jit(solution)/shard_map/ppermute | solution.py:184
  149.1 1.3 collective-permute-start.25
  150.4 2.9 collective-permute-start.2
  153.4 1.2 broadcast_select_fusion.rest_12_
  154.6 10.5 %collective-permute-start = (f32[384]{0:T(512)S(1)}, f32[384]{0:T(512)S(1)}, u32[]{:S(2)}, u32[]{:S(2)}) collective-permute-start(f32[384]{0:T(512)S(1)} %convert_multiply_fusion), channel_id=1, source_target_pairs={{0,1},{1,2},{2,3},{3,0},{4,5},{5,6},{6,7},{7,4},{8,9},{9,10},{10,1... | collective-permute-start | bytes 4616 | tf_op jit(solution)/shard_map/ppermute | solution.py:143
  165.2 1.2 broadcast_select_fusion.3.rest_4_
  166.4 1.3 collective-permute-start.17
  167.7 0.8 collective-permute-start.35
  168.5 0.7 collective-permute-start.30
  169.2 1.6 collective-permute-start.37
  170.8 1.6 collective-permute-start.16
  173.0 4.0 %multiply_convert_fusion.3 = (bf16[384,1024]{1,0:T(8,128)(2,1)}, bf16[384,1024]{1,0:T(8,128)(2,1)}, bf16[384,1024]{1,0:T(8,128)(2,1)}, bf16[384,1024]{1,0:T(8,128)(2,1)}) fusion(bf16[384,1024]{1,0:T(8,128)(2,1)S(1)} %get-tuple-element.35.rest_0_, f32[384]{0:T(512)S(1)} %convert_multiply_fusion, bf16[384,1024]{1,0:T(8,128)(2,1)} %copy-done.15, ...), kind=kLoop, calls=%fused_computation.7 | loop fusion | flops 5505024 | bytes 6292993 | tf_op jit(solution)/shard_map/convert_element_type | solution.py:205
  181.4 2.1 collective-permute-done.17
  183.4 5.1 %collective-permute-start.27 = (bf16[384,1024]{1,0:T(8,128)(2,1)S(1)}, bf16[384,1024]{1,0:T(8,128)(2,1)S(1)}, u32[]{:S(2)}, u32[]{:S(2)}) collective-permute-start(bf16[384,1024]{1,0:T(8,128)(2,1)S(1)} %get-tuple-element.35.rest_0_), channel_id=1, source_target_pairs={{0,4},{4,0},{8,12},{12,8},{1,5},{5,1},{9,13},{13,9},{2,6},{6,2},{1... | collective-permute-start | bytes 2359304 | tf_op jit(solution)/shard_map/ppermute | solution.py:89
  188.6 4.0 %collective-permute-start.28 = (bf16[384,1024]{1,0:T(8,128)(2,1)}, bf16[384,1024]{1,0:T(8,128)(2,1)S(1)}, u32[]{:S(2)}, u32[]{:S(2)}) collective-permute-start(bf16[384,1024]{1,0:T(8,128)(2,1)} %copy-done.1), channel_id=1, source_target_pairs={{0,4},{4,0},{8,12},{12,8},{1,5},{5,1},{9,13},{13,9},{2,6},{6,2},{1... | collective-permute-start | bytes 2359304 | tf_op jit(solution)/shard_map/ppermute | solution.py:89
  192.5 7.0 %collective-permute-done.30.rest_6_ = bf16[384,1024]{1,0:T(8,128)(2,1)} collective-permute-done((bf16[384,1024]{1,0:T(8,128)(2,1)S(1)}, bf16[384,1024]{1,0:T(8,128)(2,1)}, u32[]{:S(2)}, u32[]{:S(2)}) %collective-permute-start.30) | collective-permute-done | bytes 786464 | tf_op jit(solution)/shard_map/ppermute | solution.py:89
  199.6 5.1 %collective-permute-start.32 = (bf16[384,1024]{1,0:T(8,128)(2,1)S(1)}, bf16[384,1024]{1,0:T(8,128)(2,1)S(1)}, u32[]{:S(2)}, u32[]{:S(2)}) collective-permute-start(bf16[384,1024]{1,0:T(8,128)(2,1)S(1)} %broadcast_select_fusion.6.rest_8_), channel_id=1, source_target_pairs={{0,4},{4,0},{8,12},{12,8},{1,5},{5,1},{9,13},{13,9},{2,6},{6,2},{1... | collective-permute-start | bytes 2359304 | tf_op jit(solution)/shard_map/ppermute | solution.py:89
  204.7 1.3 collective-permute-start.26
  206.0 1.3 collective-permute-start.38
  207.3 4.3 %multiply_convert_fusion.1 = (bf16[384,1024]{1,0:T(8,128)(2,1)S(1)}, bf16[384,1024]{1,0:T(8,128)(2,1)}, bf16[384,1024]{1,0:T(8,128)(2,1)}, bf16[384,1024]{1,0:T(8,128)(2,1)S(1)}) fusion(bf16[384,1024]{1,0:T(8,128)(2,1)S(1)} %broadcast_select_fusion.6.rest_8_, f32[384]{0:T(512)S(1)} %collective-permute-done.1, bf16[384,1024]{1,0:T(8,128)(2,1)} %collective-permute-done.22, ...), kind=kLoop, calls=%fused_computation.5 | loop fusion | flops 6684672 | bytes 8652289 | tf_op jit(solution)/shard_map/convert_element_type | solution.py:205
  211.6 4.3 %multiply_convert_fusion.2 = (bf16[384,1024]{1,0:T(8,128)(2,1)S(1)}, bf16[384,1024]{1,0:T(8,128)(2,1)}, bf16[384,1024]{1,0:T(8,128)(2,1)}, bf16[384,1024]{1,0:T(8,128)(2,1)S(1)}) fusion(bf16[384,1024]{1,0:T(8,128)(2,1)S(1)} %broadcast_select_fusion.3.rest_4_, f32[384]{0:T(512)S(1)} %collective-permute-done, bf16[384,1024]{1,0:T(8,128)(2,1)} %collective-permute-done.4, ...), kind=kLoop, calls=%fused_computation.6 | loop fusion | flops 6684672 | bytes 8652290 | tf_op jit(solution)/shard_map/convert_element_type | solution.py:205
  216.6 9.3 %collective-permute-done.26 = bf16[384,1024]{1,0:T(8,128)(2,1)S(1)} collective-permute-done((bf16[384,1024]{1,0:T(8,128)(2,1)}, bf16[384,1024]{1,0:T(8,128)(2,1)S(1)}, u32[]{:S(2)}, u32[]{:S(2)}) %collective-permute-start.26) | collective-permute-done | bytes 786464 | tf_op jit(solution)/shard_map/ppermute | solution.py:184
  226.0 1.2 collective-permute-start.36
  227.1 15.7 %collective-permute-done.38 = bf16[384,1024]{1,0:T(8,128)(2,1)S(1)} collective-permute-done((bf16[384,1024]{1,0:T(8,128)(2,1)}, bf16[384,1024]{1,0:T(8,128)(2,1)S(1)}, u32[]{:S(2)}, u32[]{:S(2)}) %collective-permute-start.38) | collective-permute-done | bytes 786464 | tf_op jit(solution)/shard_map/ppermute | solution.py:184
  242.8 0.8 collective-permute-start.31
  243.6 3.9 %multiply_convert_fusion = (bf16[384,1024]{1,0:T(8,128)(2,1)S(1)}, bf16[384,1024]{1,0:T(8,128)(2,1)}, bf16[384,1024]{1,0:T(8,128)(2,1)}, bf16[384,1024]{1,0:T(8,128)(2,1)S(1)}) fusion(bf16[384,1024]{1,0:T(8,128)(2,1)S(1)} %broadcast_select_fusion.rest_12_, f32[384]{0:T(512)S(1)} %collective-permute-done.2, bf16[384,1024]{1,0:T(8,128)(2,1)S(1)} %collective-permute-done.38, ...), kind=kLoop, calls=%fused_computation.4 | loop fusion | flops 6684672 | bytes 8652290 | tf_op jit(solution)/shard_map/convert_element_type | solution.py:205
  247.5 1.0 pad_maximum_fusion.2
  248.6 2.5 shard_map.37.rest_0_.rest_1_.rest_2_.rest_3_
  251.1 4.5 %copy-done = bf16[1536,4096]{1,0:T(8,128)(2,1)} copy-done((bf16[1536,4096]{1,0:T(8,128)(2,1)}, bf16[1536,4096]{1,0:T(8,128)(2,1)S(1)}, u32[]{:S(2)}) %copy-start) | copy-done | bytes 12582936
  255.7 23.4 %shard_map.38.rest_4_ = f32[4096,4,1024]{2,1,0:T(4,128)} custom-call(s32[1]{0:T(128)} %bitcast.9.place_ref, f32[1]{0:T(128)} %bitcast.5.total_ref, bf16[1536,1024]{1,0:T(8,128)(2,1)S(1)} %get-tuple-element.82.left_ref, bf16[1536,4096]{1,0:T(8,128)(2,1)} %copy-done, bf16[1536,4096]{1,0:T(8,128)(2,1)} %copy-done, bf16[1536,4096]{1,0:T(8,128)(2,1)} %copy-done, ...), custom_call_target="tpu_custom_call" | custom-call | flops 12884901888 | bytes 32505856 | tf_op jit(solution)/shard_map/pallas_call | solution.py:63
  279.1 23.5 %shard_map.39.rest_4_ = f32[4096,4,1024]{2,1,0:T(4,128)} custom-call(s32[1]{0:T(128)} %bitcast.8.place_ref, f32[1]{0:T(128)} %bitcast.5.total_ref, bf16[1536,1024]{1,0:T(8,128)(2,1)S(1)} %get-tuple-element.81.left_ref, bf16[1536,4096]{1,0:T(8,128)(2,1)} %copy-done, bf16[1536,4096]{1,0:T(8,128)(2,1)} %copy-done, ...), custom_call_target="tpu_custom_call", output_to_operand_aliasing={{}: (7, {})} | custom-call | flops 12884901888 | bytes 32505856 | tf_op jit(solution)/shard_map/pallas_call | solution.py:63
  302.7 1.0 pad_maximum_fusion
  303.7 23.4 %shard_map.40.rest_4_ = f32[4096,4,1024]{2,1,0:T(4,128)} custom-call(s32[1]{0:T(128)} %bitcast.7.place_ref, f32[1]{0:T(128)} %bitcast.5.total_ref, bf16[1536,1024]{1,0:T(8,128)(2,1)S(1)} %get-tuple-element.80.left_ref, bf16[1536,4096]{1,0:T(8,128)(2,1)} %copy-done, bf16[1536,4096]{1,0:T(8,128)(2,1)} %copy-done, ...), custom_call_target="tpu_custom_call", output_to_operand_aliasing={{}: (7, {})} | custom-call | flops 12884901888 | bytes 32505856 | tf_op jit(solution)/shard_map/pallas_call | solution.py:63
  327.1 23.4 %shard_map.41 = f32[4096,4,1024]{2,1,0:T(4,128)} custom-call(s32[1]{0:T(128)} %bitcast.place_ref, f32[1]{0:T(128)} %bitcast.5.total_ref, bf16[1536,1024]{1,0:T(8,128)(2,1)S(1)} %get-tuple-element.79.left_ref, bf16[1536,4096]{1,0:T(8,128)(2,1)} %copy-done, bf16[1536,4096]{1,0:T(8,128)(2,1)} %copy-done, ...), custom_call_target="tpu_custom_call", output_to_operand_aliasing={{}: (7, {})} | custom-call | flops 12884901888 | bytes 32505856 | tf_op jit(solution)/shard_map/pallas_call | solution.py:63
  (94 shorter events, 5.7 us)
Async XLA Ops:
  6.5 52.3 %copy-start.15 = (bf16[384,1024]{1,0:T(8,128)(2,1)}, bf16[384,1024]{1,0:T(8,128)(2,1)S(1)}, u32[]{:S(2)}) copy-start(bf16[384,1024]{1,0:T(8,128)(2,1)S(1)} %get-tuple-element.36) | copy-start | bytes 2359300
  6.5 18.6 %collective-permute-start.6 = (bf16[384,1024]{1,0:T(8,128)(2,1)}, bf16[384,1024]{1,0:T(8,128)(2,1)S(1)}, u32[]{:S(2)}, u32[]{:S(2)}) collective-permute-start(bf16[384,1024]{1,0:T(8,128)(2,1)} %get-tuple-element.32), channel_id=1, source_target_pairs={{1,0},{2,1},{3,2},{5,4},{6,5},{7,6},{9,8},{10,9},{11,10},{13,12},{... | collective-permute-start | bytes 2359304 | tf_op jit(solution)/shard_map/ppermute | solution.py:190
  8.6 20.6 %collective-permute-start.3 = (bf16[384,1024]{1,0:T(8,128)(2,1)}, bf16[384,1024]{1,0:T(8,128)(2,1)}, u32[]{:S(2)}, u32[]{:S(2)}) collective-permute-start(bf16[384,1024]{1,0:T(8,128)(2,1)} %get-tuple-element.34), channel_id=1, source_target_pairs={{0,1},{1,2},{2,3},{4,5},{5,6},{6,7},{8,9},{9,10},{10,11},{12,13},{... | collective-permute-start | bytes 2359304 | tf_op jit(solution)/shard_map/ppermute | solution.py:184
  9.9 35.9 %collective-permute-start.15 = (bf16[384,1024]{1,0:T(8,128)(2,1)S(1)}, bf16[384,1024]{1,0:T(8,128)(2,1)}, u32[]{:S(2)}, u32[]{:S(2)}) collective-permute-start(bf16[384,1024]{1,0:T(8,128)(2,1)S(1)} %get-tuple-element.36), channel_id=1, source_target_pairs={{0,1},{1,2},{2,3},{4,5},{5,6},{6,7},{8,9},{9,10},{10,11},{12,13},{... | collective-permute-start | bytes 2359304 | tf_op jit(solution)/shard_map/ppermute | solution.py:184
  11.2 35.8 %collective-permute-start.9 = (bf16[384,1024]{1,0:T(8,128)(2,1)S(1)}, bf16[384,1024]{1,0:T(8,128)(2,1)S(1)}, u32[]{:S(2)}, u32[]{:S(2)}) collective-permute-start(bf16[384,1024]{1,0:T(8,128)(2,1)S(1)} %get-tuple-element.36), channel_id=1, source_target_pairs={{1,0},{2,1},{3,2},{5,4},{6,5},{7,6},{9,8},{10,9},{11,10},{13,12},{... | collective-permute-start | bytes 2359304 | tf_op jit(solution)/shard_map/ppermute | solution.py:190
  25.1 38.7 %copy-start.24 = (bf16[384,1024]{1,0:T(8,128)(2,1)}, bf16[384,1024]{1,0:T(8,128)(2,1)S(1)}, u32[]{:S(2)}) copy-start(bf16[384,1024]{1,0:T(8,128)(2,1)S(1)} %collective-permute-done.6) | copy-start | bytes 2359300
  25.1 33.7 %collective-permute-start.7 = (bf16[384,1024]{1,0:T(8,128)(2,1)}, bf16[384,1024]{1,0:T(8,128)(2,1)S(1)}, u32[]{:S(2)}, u32[]{:S(2)}) collective-permute-start(bf16[384,1024]{1,0:T(8,128)(2,1)} %get-tuple-element.34), channel_id=1, source_target_pairs={{1,0},{2,1},{3,2},{5,4},{6,5},{7,6},{9,8},{10,9},{11,10},{13,12},{... | collective-permute-start | bytes 2359304 | tf_op jit(solution)/shard_map/ppermute | solution.py:190
  29.3 35.8 %collective-permute-start.4 = (bf16[384,1024]{1,0:T(8,128)(2,1)}, bf16[384,1024]{1,0:T(8,128)(2,1)}, u32[]{:S(2)}, u32[]{:S(2)}) collective-permute-start(bf16[384,1024]{1,0:T(8,128)(2,1)} %get-tuple-element.32), channel_id=1, source_target_pairs={{0,1},{1,2},{2,3},{4,5},{5,6},{6,7},{8,9},{9,10},{10,11},{12,13},{... | collective-permute-start | bytes 2359304 | tf_op jit(solution)/shard_map/ppermute | solution.py:184
  45.8 33.7 %collective-permute-start.20 = (bf16[384,1024]{1,0:T(8,128)(2,1)}, bf16[384,1024]{1,0:T(8,128)(2,1)}, u32[]{:S(2)}, u32[]{:S(2)}) collective-permute-start(bf16[384,1024]{1,0:T(8,128)(2,1)} %collective-permute-done.15), channel_id=1, source_target_pairs={{1,2},{2,3},{5,6},{6,7},{9,10},{10,11},{13,14},{14,15},{17,18},{18... | collective-permute-start | bytes 2359304 | tf_op jit(solution)/shard_map/ppermute | solution.py:184
  47.1 33.7 %copy-start.16 = (bf16[384,1024]{1,0:T(8,128)(2,1)}, bf16[384,1024]{1,0:T(8,128)(2,1)S(1)}, u32[]{:S(2)}) copy-start(bf16[384,1024]{1,0:T(8,128)(2,1)S(1)} %collective-permute-done.9) | copy-start | bytes 2359300
  47.1 33.7 %collective-permute-start.12 = (bf16[384,1024]{1,0:T(8,128)(2,1)S(1)}, bf16[384,1024]{1,0:T(8,128)(2,1)}, u32[]{:S(2)}, u32[]{:S(2)}) collective-permute-start(bf16[384,1024]{1,0:T(8,128)(2,1)S(1)} %collective-permute-done.9), channel_id=1, source_target_pairs={{1,0},{2,1},{5,4},{6,5},{9,8},{10,9},{13,12},{14,13},{17,16},{18,1... | collective-permute-start | bytes 2359304 | tf_op jit(solution)/shard_map/ppermute | solution.py:190
  58.8 95.8 %copy-start.18 = (bf16[384,1024]{1,0:T(8,128)(2,1)}, bf16[384,1024]{1,0:T(8,128)(2,1)S(1)}, u32[]{:S(2)}) copy-start(bf16[384,1024]{1,0:T(8,128)(2,1)S(1)} %collective-permute-done.7) | copy-start | bytes 2359300
  58.8 24.0 %collective-permute-start.8 = (bf16[384,1024]{1,0:T(8,128)(2,1)S(1)}, bf16[384,1024]{1,0:T(8,128)(2,1)}, u32[]{:S(2)}, u32[]{:S(2)}) collective-permute-start(bf16[384,1024]{1,0:T(8,128)(2,1)S(1)} %get-tuple-element.35.rest_0_), channel_id=1, source_target_pairs={{1,0},{2,1},{3,2},{5,4},{6,5},{7,6},{9,8},{10,9},{11,10},{13,12},{... | collective-permute-start | bytes 2359304 | tf_op jit(solution)/shard_map/ppermute | solution.py:190
  63.8 21.8 %collective-permute-start.23 = (bf16[384,1024]{1,0:T(8,128)(2,1)S(1)}, bf16[384,1024]{1,0:T(8,128)(2,1)S(1)}, u32[]{:S(2)}, u32[]{:S(2)}) collective-permute-start(bf16[384,1024]{1,0:T(8,128)(2,1)S(1)} %get-tuple-element.35.rest_0_), channel_id=1, source_target_pairs={{0,8},{4,12},{8,0},{12,4},{1,9},{5,13},{9,1},{13,5},{2,10},{6,14},... | collective-permute-start | bytes 2359304 | tf_op jit(solution)/shard_map/ppermute | solution.py:89
  65.0 49.4 %collective-permute-start.5 = (bf16[384,1024]{1,0:T(8,128)(2,1)S(1)}, bf16[384,1024]{1,0:T(8,128)(2,1)S(1)}, u32[]{:S(2)}, u32[]{:S(2)}) collective-permute-start(bf16[384,1024]{1,0:T(8,128)(2,1)S(1)} %get-tuple-element.35.rest_0_), channel_id=1, source_target_pairs={{0,1},{1,2},{2,3},{4,5},{5,6},{6,7},{8,9},{9,10},{10,11},{12,13},{... | collective-permute-start | bytes 2359304 | tf_op jit(solution)/shard_map/ppermute | solution.py:184
  79.5 33.6 %collective-permute-start.18 = (bf16[384,1024]{1,0:T(8,128)(2,1)}, bf16[384,1024]{1,0:T(8,128)(2,1)S(1)}, u32[]{:S(2)}, u32[]{:S(2)}) collective-permute-start(bf16[384,1024]{1,0:T(8,128)(2,1)} %collective-permute-done.4), channel_id=1, source_target_pairs={{1,2},{2,3},{5,6},{6,7},{9,10},{10,11},{13,14},{14,15},{17,18},{18... | collective-permute-start | bytes 2359304 | tf_op jit(solution)/shard_map/ppermute | solution.py:184
  80.8 3.2 collective-permute-start.10
  82.8 31.6 %collective-permute-start.21 = (bf16[384,1024]{1,0:T(8,128)(2,1)S(1)}, bf16[384,1024]{1,0:T(8,128)(2,1)S(1)}, u32[]{:S(2)}, u32[]{:S(2)}) collective-permute-start(bf16[384,1024]{1,0:T(8,128)(2,1)S(1)} %broadcast_select_fusion.6.rest_8_), channel_id=1, source_target_pairs={{0,8},{4,12},{8,0},{12,4},{1,9},{5,13},{9,1},{13,5},{2,10},{6,14},... | collective-permute-start | bytes 2359304 | tf_op jit(solution)/shard_map/ppermute | solution.py:89
  84.0 66.4 %copy-start.23 = (bf16[384,1024]{1,0:T(8,128)(2,1)}, bf16[384,1024]{1,0:T(8,128)(2,1)S(1)}, u32[]{:S(2)}) copy-start(bf16[384,1024]{1,0:T(8,128)(2,1)S(1)} %collective-permute-done.10) | copy-start | bytes 2359300
  84.1 34.5 %collective-permute-start.11 = (bf16[384,1024]{1,0:T(8,128)(2,1)}, bf16[384,1024]{1,0:T(8,128)(2,1)}, u32[]{:S(2)}, u32[]{:S(2)}) collective-permute-start(bf16[384,1024]{1,0:T(8,128)(2,1)} %collective-permute-done.8), channel_id=1, source_target_pairs={{1,0},{2,1},{5,4},{6,5},{9,8},{10,9},{13,12},{14,13},{17,16},{18,1... | collective-permute-start | bytes 2359304 | tf_op jit(solution)/shard_map/ppermute | solution.py:190
  85.6 67.8 %copy-start.1 = (bf16[384,1024]{1,0:T(8,128)(2,1)}, bf16[384,1024]{1,0:T(8,128)(2,1)S(1)}, u32[]{:S(2)}) copy-start(bf16[384,1024]{1,0:T(8,128)(2,1)S(1)} %collective-permute-done.23.rest_2_) | copy-start | bytes 2359300
  85.6 32.9 %collective-permute-start.13 = (bf16[384,1024]{1,0:T(8,128)(2,1)S(1)}, bf16[384,1024]{1,0:T(8,128)(2,1)S(1)}, u32[]{:S(2)}, u32[]{:S(2)}) collective-permute-start(bf16[384,1024]{1,0:T(8,128)(2,1)S(1)} %collective-permute-done.10), channel_id=1, source_target_pairs={{1,0},{5,4},{9,8},{13,12},{17,16},{21,20},{25,24},{29,28}} | collective-permute-start | bytes 2359304 | tf_op jit(solution)/shard_map/ppermute | solution.py:190
  113.1 36.0 %copy-start.22 = (bf16[384,1024]{1,0:T(8,128)(2,1)}, bf16[384,1024]{1,0:T(8,128)(2,1)S(1)}, u32[]{:S(2)}) copy-start(bf16[384,1024]{1,0:T(8,128)(2,1)S(1)} %collective-permute-done.18) | copy-start | bytes 2359300
  113.1 19.1 %collective-permute-start.24 = (bf16[384,1024]{1,0:T(8,128)(2,1)S(1)}, bf16[384,1024]{1,0:T(8,128)(2,1)S(1)}, u32[]{:S(2)}, u32[]{:S(2)}) collective-permute-start(bf16[384,1024]{1,0:T(8,128)(2,1)S(1)} %collective-permute-done.18), channel_id=1, source_target_pairs={{2,3},{6,7},{10,11},{14,15},{18,19},{22,23},{26,27},{30,31}} | collective-permute-start | bytes 2359304 | tf_op jit(solution)/shard_map/ppermute | solution.py:184
  114.4 2.5 copy-start.20
  115.6 33.5 %collective-permute-start.22 = (bf16[384,1024]{1,0:T(8,128)(2,1)S(1)}, bf16[384,1024]{1,0:T(8,128)(2,1)}, u32[]{:S(2)}, u32[]{:S(2)}) collective-permute-start(bf16[384,1024]{1,0:T(8,128)(2,1)S(1)} %collective-permute-done.5), channel_id=1, source_target_pairs={{1,2},{2,3},{5,6},{6,7},{9,10},{10,11},{13,14},{14,15},{17,18},{18... | collective-permute-start | bytes 2359304 | tf_op jit(solution)/shard_map/ppermute | solution.py:184
  116.9 37.7 %collective-permute-start.19 = (bf16[384,1024]{1,0:T(8,128)(2,1)}, bf16[384,1024]{1,0:T(8,128)(2,1)}, u32[]{:S(2)}, u32[]{:S(2)}) collective-permute-start(bf16[384,1024]{1,0:T(8,128)(2,1)} %copy-done.24), channel_id=1, source_target_pairs={{1,0},{2,1},{5,4},{6,5},{9,8},{10,9},{13,12},{14,13},{17,16},{18,1... | collective-permute-start | bytes 2359304 | tf_op jit(solution)/shard_map/ppermute | solution.py:190
  118.5 34.9 %copy-start.25 = (bf16[384,1024]{1,0:T(8,128)(2,1)}, bf16[384,1024]{1,0:T(8,128)(2,1)S(1)}, u32[]{:S(2)}) copy-start(bf16[384,1024]{1,0:T(8,128)(2,1)S(1)} %collective-permute-done.13) | copy-start | bytes 2359300
  118.5 47.9 %collective-permute-start.14 = (bf16[384,1024]{1,0:T(8,128)(2,1)}, bf16[384,1024]{1,0:T(8,128)(2,1)}, u32[]{:S(2)}, u32[]{:S(2)}) collective-permute-start(bf16[384,1024]{1,0:T(8,128)(2,1)} %collective-permute-done.11), channel_id=1, source_target_pairs={{1,0},{5,4},{9,8},{13,12},{17,16},{21,20},{25,24},{29,28}} | collective-permute-start | bytes 2359304 | tf_op jit(solution)/shard_map/ppermute | solution.py:190
  132.2 21.2 %copy-start.26 = (bf16[384,1024]{1,0:T(8,128)(2,1)}, bf16[384,1024]{1,0:T(8,128)(2,1)S(1)}, u32[]{:S(2)}) copy-start(bf16[384,1024]{1,0:T(8,128)(2,1)S(1)} %collective-permute-done.24) | copy-start | bytes 2359300
  149.1 21.7 %collective-permute-start.25 = (bf16[384,1024]{1,0:T(8,128)(2,1)}, bf16[384,1024]{1,0:T(8,128)(2,1)}, u32[]{:S(2)}, u32[]{:S(2)}) collective-permute-start(bf16[384,1024]{1,0:T(8,128)(2,1)} %collective-permute-done.22), channel_id=1, source_target_pairs={{2,3},{6,7},{10,11},{14,15},{18,19},{22,23},{26,27},{30,31}} | collective-permute-start | bytes 2359304 | tf_op jit(solution)/shard_map/ppermute | solution.py:184
  150.4 17.3 %collective-permute-start.2 = (f32[384]{0:T(512)S(1)}, f32[384]{0:T(512)S(1)}, u32[]{:S(2)}, u32[]{:S(2)}) collective-permute-start(f32[384]{0:T(512)S(1)} %convert_multiply_fusion), channel_id=1, source_target_pairs={{0,3},{1,0},{2,1},{3,2},{4,7},{5,4},{6,5},{7,6},{8,11},{9,8},{10,9... | collective-permute-start | bytes 4616 | tf_op jit(solution)/shard_map/ppermute | solution.py:143
  153.4 15.1 %collective-permute-start.1 = (f32[384]{0:T(512)S(1)}, f32[384]{0:T(512)S(1)}, u32[]{:S(2)}, u32[]{:S(2)}) collective-permute-start(f32[384]{0:T(512)S(1)} %convert_multiply_fusion), channel_id=1, source_target_pairs={{0,2},{1,3},{2,0},{3,1},{4,6},{5,7},{6,4},{7,5},{8,10},{9,11},{10,... | collective-permute-start | bytes 4616 | tf_op jit(solution)/shard_map/ppermute | solution.py:143
  154.6 14.6 %collective-permute-start = (f32[384]{0:T(512)S(1)}, f32[384]{0:T(512)S(1)}, u32[]{:S(2)}, u32[]{:S(2)}) collective-permute-start(f32[384]{0:T(512)S(1)} %convert_multiply_fusion), channel_id=1, source_target_pairs={{0,1},{1,2},{2,3},{3,0},{4,5},{5,6},{6,7},{7,4},{8,9},{9,10},{10,1... | collective-permute-start | bytes 4616 | tf_op jit(solution)/shard_map/ppermute | solution.py:143
  166.4 17.1 %collective-permute-start.17 = (bf16[384,1024]{1,0:T(8,128)(2,1)}, bf16[384,1024]{1,0:T(8,128)(2,1)}, u32[]{:S(2)}, u32[]{:S(2)}) collective-permute-start(bf16[384,1024]{1,0:T(8,128)(2,1)} %collective-permute-done.3), channel_id=1, source_target_pairs={{1,2},{2,3},{5,6},{6,7},{9,10},{10,11},{13,14},{14,15},{17,18},{18... | collective-permute-start | bytes 2359304 | tf_op jit(solution)/shard_map/ppermute | solution.py:184
  167.7 20.9 %collective-permute-start.35 = (bf16[384,1024]{1,0:T(8,128)(2,1)S(1)}, bf16[384,1024]{1,0:T(8,128)(2,1)}, u32[]{:S(2)}, u32[]{:S(2)}) collective-permute-start(bf16[384,1024]{1,0:T(8,128)(2,1)S(1)} %broadcast_select_fusion.rest_12_), channel_id=1, source_target_pairs={{0,8},{4,12},{8,0},{12,4},{1,9},{5,13},{9,1},{13,5},{2,10},{6,14},... | collective-permute-start | bytes 2359304 | tf_op jit(solution)/shard_map/ppermute | solution.py:89
  168.5 31.1 %collective-permute-start.30 = (bf16[384,1024]{1,0:T(8,128)(2,1)S(1)}, bf16[384,1024]{1,0:T(8,128)(2,1)}, u32[]{:S(2)}, u32[]{:S(2)}) collective-permute-start(bf16[384,1024]{1,0:T(8,128)(2,1)S(1)} %broadcast_select_fusion.3.rest_4_), channel_id=1, source_target_pairs={{0,8},{4,12},{8,0},{12,4},{1,9},{5,13},{9,1},{13,5},{2,10},{6,14},... | collective-permute-start | bytes 2359304 | tf_op jit(solution)/shard_map/ppermute | solution.py:89
  169.2 35.4 %collective-permute-start.37 = (bf16[384,1024]{1,0:T(8,128)(2,1)}, bf16[384,1024]{1,0:T(8,128)(2,1)}, u32[]{:S(2)}, u32[]{:S(2)}) collective-permute-start(bf16[384,1024]{1,0:T(8,128)(2,1)} %collective-permute-done.19), channel_id=1, source_target_pairs={{1,0},{5,4},{9,8},{13,12},{17,16},{21,20},{25,24},{29,28}} | collective-permute-start | bytes 2359304 | tf_op jit(solution)/shard_map/ppermute | solution.py:190
  170.8 35.2 %collective-permute-start.16 = (bf16[384,1024]{1,0:T(8,128)(2,1)}, bf16[384,1024]{1,0:T(8,128)(2,1)}, u32[]{:S(2)}, u32[]{:S(2)}) collective-permute-start(bf16[384,1024]{1,0:T(8,128)(2,1)} %collective-permute-done.12), channel_id=1, source_target_pairs={{1,0},{5,4},{9,8},{13,12},{17,16},{21,20},{25,24},{29,28}} | collective-permute-start | bytes 2359304 | tf_op jit(solution)/shard_map/ppermute | solution.py:190
  181.4 30.2 %copy-start.21 = (bf16[384,1024]{1,0:T(8,128)(2,1)S(1)}, bf16[384,1024]{1,0:T(8,128)(2,1)}, u32[]{:S(2)}) copy-start(bf16[384,1024]{1,0:T(8,128)(2,1)} %copy-done.20) | copy-start | bytes 2359300
  183.4 32.5 %collective-permute-start.27 = (bf16[384,1024]{1,0:T(8,128)(2,1)S(1)}, bf16[384,1024]{1,0:T(8,128)(2,1)S(1)}, u32[]{:S(2)}, u32[]{:S(2)}) collective-permute-start(bf16[384,1024]{1,0:T(8,128)(2,1)S(1)} %get-tuple-element.35.rest_0_), channel_id=1, source_target_pairs={{0,4},{4,0},{8,12},{12,8},{1,5},{5,1},{9,13},{13,9},{2,6},{6,2},{1... | collective-permute-start | bytes 2359304 | tf_op jit(solution)/shard_map/ppermute | solution.py:89
  188.6 27.5 %collective-permute-start.28 = (bf16[384,1024]{1,0:T(8,128)(2,1)}, bf16[384,1024]{1,0:T(8,128)(2,1)S(1)}, u32[]{:S(2)}, u32[]{:S(2)}) collective-permute-start(bf16[384,1024]{1,0:T(8,128)(2,1)} %copy-done.1), channel_id=1, source_target_pairs={{0,4},{4,0},{8,12},{12,8},{1,5},{5,1},{9,13},{13,9},{2,6},{6,2},{1... | collective-permute-start | bytes 2359304 | tf_op jit(solution)/shard_map/ppermute | solution.py:89
  199.6 17.0 %collective-permute-start.32 = (bf16[384,1024]{1,0:T(8,128)(2,1)S(1)}, bf16[384,1024]{1,0:T(8,128)(2,1)S(1)}, u32[]{:S(2)}, u32[]{:S(2)}) collective-permute-start(bf16[384,1024]{1,0:T(8,128)(2,1)S(1)} %broadcast_select_fusion.6.rest_8_), channel_id=1, source_target_pairs={{0,4},{4,0},{8,12},{12,8},{1,5},{5,1},{9,13},{13,9},{2,6},{6,2},{1... | collective-permute-start | bytes 2359304 | tf_op jit(solution)/shard_map/ppermute | solution.py:89
  204.7 21.3 %collective-permute-start.26 = (bf16[384,1024]{1,0:T(8,128)(2,1)}, bf16[384,1024]{1,0:T(8,128)(2,1)S(1)}, u32[]{:S(2)}, u32[]{:S(2)}) collective-permute-start(bf16[384,1024]{1,0:T(8,128)(2,1)} %collective-permute-done.20), channel_id=1, source_target_pairs={{2,3},{6,7},{10,11},{14,15},{18,19},{22,23},{26,27},{30,31}} | collective-permute-start | bytes 2359304 | tf_op jit(solution)/shard_map/ppermute | solution.py:184
  206.0 36.8 %collective-permute-start.38 = (bf16[384,1024]{1,0:T(8,128)(2,1)}, bf16[384,1024]{1,0:T(8,128)(2,1)S(1)}, u32[]{:S(2)}, u32[]{:S(2)}) collective-permute-start(bf16[384,1024]{1,0:T(8,128)(2,1)} %collective-permute-done.17), channel_id=1, source_target_pairs={{2,3},{6,7},{10,11},{14,15},{18,19},{22,23},{26,27},{30,31}} | collective-permute-start | bytes 2359304 | tf_op jit(solution)/shard_map/ppermute | solution.py:184
  211.6 4.3 %copy-start.4 = (bf16[384,1024]{1,0:T(8,128)(2,1)S(1)}, bf16[384,1024]{1,0:T(8,128)(2,1)}, u32[]{:S(2)}) copy-start(bf16[384,1024]{1,0:T(8,128)(2,1)} %copy-done.3) | copy-start | bytes 2359300
  211.6 32.0 %copy-start.17 = (bf16[384,1024]{1,0:T(8,128)(2,1)S(1)}, bf16[384,1024]{1,0:T(8,128)(2,1)}, u32[]{:S(2)}) copy-start(bf16[384,1024]{1,0:T(8,128)(2,1)} %copy-done.16) | copy-start | bytes 2359300
  211.6 32.0 %copy-start.19 = (bf16[384,1024]{1,0:T(8,128)(2,1)S(1)}, bf16[384,1024]{1,0:T(8,128)(2,1)}, u32[]{:S(2)}) copy-start(bf16[384,1024]{1,0:T(8,128)(2,1)} %copy-done.18) | copy-start | bytes 2359300
  215.9 31.5 %copy-start.7 = (bf16[384,1024]{1,0:T(8,128)(2,1)S(1)}, bf16[384,1024]{1,0:T(8,128)(2,1)}, u32[]{:S(2)}) copy-start(bf16[384,1024]{1,0:T(8,128)(2,1)} %get-tuple-element.63) | copy-start | bytes 2359300
  215.9 31.5 %copy-start.8 = (bf16[384,1024]{1,0:T(8,128)(2,1)S(1)}, bf16[384,1024]{1,0:T(8,128)(2,1)}, u32[]{:S(2)}) copy-start(bf16[384,1024]{1,0:T(8,128)(2,1)} %get-tuple-element.66) | copy-start | bytes 2359300
  215.9 32.5 %collective-permute-start.33 = (bf16[384,1024]{1,0:T(8,128)(2,1)S(1)}, bf16[384,1024]{1,0:T(8,128)(2,1)S(1)}, u32[]{:S(2)}, u32[]{:S(2)}) collective-permute-start(bf16[384,1024]{1,0:T(8,128)(2,1)S(1)} %copy-done.4), channel_id=1, source_target_pairs={{0,4},{4,0},{8,12},{12,8},{1,5},{5,1},{9,13},{13,9},{2,6},{6,2},{1... | collective-permute-start | bytes 2359304 | tf_op jit(solution)/shard_map/ppermute | solution.py:89
  216.0 32.4 %collective-permute-start.34 = (bf16[384,1024]{1,0:T(8,128)(2,1)S(1)}, bf16[384,1024]{1,0:T(8,128)(2,1)S(1)}, u32[]{:S(2)}, u32[]{:S(2)}) collective-permute-start(bf16[384,1024]{1,0:T(8,128)(2,1)S(1)} %broadcast_select_fusion.rest_12_), channel_id=1, source_target_pairs={{0,4},{4,0},{8,12},{12,8},{1,5},{5,1},{9,13},{13,9},{2,6},{6,2},{1... | collective-permute-start | bytes 2359304 | tf_op jit(solution)/shard_map/ppermute | solution.py:89
  216.5 32.0 %collective-permute-start.29 = (bf16[384,1024]{1,0:T(8,128)(2,1)S(1)}, bf16[384,1024]{1,0:T(8,128)(2,1)S(1)}, u32[]{:S(2)}, u32[]{:S(2)}) collective-permute-start(bf16[384,1024]{1,0:T(8,128)(2,1)S(1)} %broadcast_select_fusion.3.rest_4_), channel_id=1, source_target_pairs={{0,4},{4,0},{8,12},{12,8},{1,5},{5,1},{9,13},{13,9},{2,6},{6,2},{1... | collective-permute-start | bytes 2359304 | tf_op jit(solution)/shard_map/ppermute | solution.py:89
  226.0 22.5 %collective-permute-start.36 = (bf16[384,1024]{1,0:T(8,128)(2,1)}, bf16[384,1024]{1,0:T(8,128)(2,1)S(1)}, u32[]{:S(2)}, u32[]{:S(2)}) collective-permute-start(bf16[384,1024]{1,0:T(8,128)(2,1)} %collective-permute-done.35.rest_14_), channel_id=1, source_target_pairs={{0,4},{4,0},{8,12},{12,8},{1,5},{5,1},{9,13},{13,9},{2,6},{6,2},{1... | collective-permute-start | bytes 2359304 | tf_op jit(solution)/shard_map/ppermute | solution.py:89
  242.8 5.7 %collective-permute-start.31 = (bf16[384,1024]{1,0:T(8,128)(2,1)}, bf16[384,1024]{1,0:T(8,128)(2,1)S(1)}, u32[]{:S(2)}, u32[]{:S(2)}) collective-permute-start(bf16[384,1024]{1,0:T(8,128)(2,1)} %collective-permute-done.30.rest_6_), channel_id=1, source_target_pairs={{0,4},{4,0},{8,12},{12,8},{1,5},{5,1},{9,13},{13,9},{2,6},{6,2},{1... | collective-permute-start | bytes 2359304 | tf_op jit(solution)/shard_map/ppermute | solution.py:89
  251.1 4.6 %copy-start = (bf16[1536,4096]{1,0:T(8,128)(2,1)}, bf16[1536,4096]{1,0:T(8,128)(2,1)S(1)}, u32[]{:S(2)}) copy-start(bf16[1536,4096]{1,0:T(8,128)(2,1)S(1)} %shard_map.37.rest_0_.rest_1_.rest_2_.rest_3_) | copy-start | bytes 37748740
  279.0 23.6 %copy-start.5 = (bf16[384,1024]{1,0:T(8,128)(2,1)S(1)}, bf16[384,1024]{1,0:T(8,128)(2,1)}, u32[]{:S(2)}) copy-start(bf16[384,1024]{1,0:T(8,128)(2,1)} %get-tuple-element.64) | copy-start | bytes 2359300
  279.0 23.6 %copy-start.6 = (bf16[384,1024]{1,0:T(8,128)(2,1)S(1)}, bf16[384,1024]{1,0:T(8,128)(2,1)}, u32[]{:S(2)}) copy-start(bf16[384,1024]{1,0:T(8,128)(2,1)} %get-tuple-element.65) | copy-start | bytes 2359300
  279.0 23.6 %copy-start.9 = (bf16[384,1024]{1,0:T(8,128)(2,1)S(1)}, bf16[384,1024]{1,0:T(8,128)(2,1)}, u32[]{:S(2)}) copy-start(bf16[384,1024]{1,0:T(8,128)(2,1)} %get-tuple-element.72) | copy-start | bytes 2359300
  279.1 23.6 %copy-start.10 = (bf16[384,1024]{1,0:T(8,128)(2,1)S(1)}, bf16[384,1024]{1,0:T(8,128)(2,1)}, u32[]{:S(2)}) copy-start(bf16[384,1024]{1,0:T(8,128)(2,1)} %get-tuple-element.73) | copy-start | bytes 2359300
  279.1 23.6 %copy-start.11 = (bf16[384,1024]{1,0:T(8,128)(2,1)S(1)}, bf16[384,1024]{1,0:T(8,128)(2,1)}, u32[]{:S(2)}) copy-start(bf16[384,1024]{1,0:T(8,128)(2,1)} %get-tuple-element.68) | copy-start | bytes 2359300
  279.1 23.6 %copy-start.12 = (bf16[384,1024]{1,0:T(8,128)(2,1)S(1)}, bf16[384,1024]{1,0:T(8,128)(2,1)}, u32[]{:S(2)}) copy-start(bf16[384,1024]{1,0:T(8,128)(2,1)} %get-tuple-element.69) | copy-start | bytes 2359300
  279.1 23.6 %copy-start.13 = (bf16[384,1024]{1,0:T(8,128)(2,1)S(1)}, bf16[384,1024]{1,0:T(8,128)(2,1)}, u32[]{:S(2)}) copy-start(bf16[384,1024]{1,0:T(8,128)(2,1)} %get-tuple-element.76) | copy-start | bytes 2359300
  279.1 23.6 %copy-start.14 = (bf16[384,1024]{1,0:T(8,128)(2,1)S(1)}, bf16[384,1024]{1,0:T(8,128)(2,1)}, u32[]{:S(2)}) copy-start(bf16[384,1024]{1,0:T(8,128)(2,1)} %get-tuple-element.77) | copy-start | bytes 2359300
  (2 other events, 2.3 us)
